TPU v7x, 32 devices: a whole 2x2x4 slice. The times are simulated.
32 devices in a mesh: groups: 2 (over y), tiles: 4 (over z), heads: 2 (over x), cfg: 2 (over core).
Axes of the slice: x: 2, y: 2, z: 4, core: 2. Of those that a mesh axis runs over, the one named last changes fastest.
Arguments:
- latents: bfloat16 [6144, 3072], P(('groups', 'tiles'), ('heads', 'cfg')), parts along dimension 0, may hold values from -6 to 6
- modulation: float32 [6, 3072], P('groups'), parts along dimension 0, may hold values from -3 to 3
- qkv_weight: bfloat16 [3072, 1536], P(None, ('heads', 'cfg')), may hold values from -0.109375 to 0.109375
- query_gain: float32 [128], replicated, may hold values from 0.25 to 1.75
- key_gain: float32 [128], replicated, may hold values from 0.25 to 1.75
- text_kv: bfloat16 [512, 1024], P('groups', ('heads', 'cfg')), parts along dimension 0, may hold values from -72 to 72
- text_len: int32 [2], P('groups'), parts along dimension 0, may hold values from 128 to 256
- tile_ids: int32 [16], P(('groups', 'tiles')), parts along dimension 0, may hold values from 0 to 7, as said below
- windows: int32 [16, 27], P('groups'), parts along dimension 0, may hold values from 0 to 7, as said below
- proj_weight: bfloat16 [512, 3072], P(None, ('heads', 'cfg')), may hold values from -0.25 to 0.25
Outputs:
- updated: bfloat16 [6144, 3072], P(('groups', 'tiles'), ('heads', 'cfg')), parts along dimension 0
There are 2 independent parts, one for each index of `groups`. A program takes and returns all parts, laid end to end along the dimension named above; an argument that names none is the same for every part. Nothing has to cross between parts.
Inputs may be any that keep to these rules, and one draw needn't show every extreme that they name: Every entry of windows[t] names a tile at most one tile away from t along each dimension of the 2 x 2 x 2 tile grid, tile id (i * 2 + h) * 2 + w; entry 13 is t itself, and entries that name no other tile repeat t. `tile_ids`: slot s holds a tile id from (s // 2) * 2 to (s // 2) * 2 + 1; every id appears once.
All inputs are finite; a program needn't handle non-finite values.
Results may differ from a plain program's by a relative error of at most 0.0033.
The roundings to bfloat16 on the way count: a program that leaves them out, or rounds other values in their place, can miss the bound.
Values may be sent and summed in bfloat16 or wider, within the bound.
No kernel may reach another device: no remote copies, remote signals or barrier semaphores. Data moves between devices by JAX's collectives and lax.ppermute only.
A program may use at most 64 MiB of HBM per device.

v0:
```python
import math

import jax
import jax.numpy as jnp
from jax import lax
from jax.sharding import PartitionSpec as P

HD = 128
TILE = 384
TXT = 256


epsilon = 1e-06


def rms_norm(values, gain):
    return values * lax.rsqrt(jnp.mean(values * values, axis=-1, keepdims=True) + epsilon) * gain


def body(
    latents,
    modulation,
    qkv_weight,
    query_gain,
    key_gain,
    text_kv,
    text_len,
    tile_ids,
    windows,
    proj_weight,
):
    tok_rows = latents.shape[0]
    per_dev = tile_ids.shape[0]
    gathered = lax.all_gather(latents, ("heads", "cfg"), axis=1, tiled=True)
    rows = gathered.astype(jnp.float32)
    average = jnp.mean(rows, axis=-1, keepdims=True)
    centred = rows - average
    spread = jnp.mean(centred * centred, axis=-1, keepdims=True)
    modulated = (
        centred * lax.rsqrt(spread + epsilon) * (1.0 + modulation[1]) + modulation[0]
    ).astype(jnp.bfloat16)
    projected = jnp.dot(modulated, qkv_weight, preferred_element_type=jnp.float32).reshape(
        tok_rows, 3, HD
    )
    queries = rms_norm(projected[:, 0], query_gain).astype(jnp.bfloat16)
    keys_own = rms_norm(projected[:, 1], key_gain).astype(jnp.bfloat16)
    values_own = projected[:, 2].astype(jnp.bfloat16)
    text_pair = text_kv.reshape(TXT, 2, HD)
    text_keys = text_pair[:, 0]
    text_values = text_pair[:, 1]
    factor = 1.0 / math.sqrt(HD)
    text_scores = jnp.dot(queries, text_keys.T, preferred_element_type=jnp.float32) * factor
    text_live = jnp.arange(TXT, dtype=jnp.int32) < text_len[0]
    text_scores = jnp.where(text_live[None, :], text_scores, -jnp.inf)
    own_marks = windows[tile_ids] + 1
    tile_marks = tile_ids + 1
    text_top = jnp.max(text_scores, axis=1)
    text_exp = jnp.exp(text_scores - text_top[:, None])
    start_state = (
        text_top,
        jnp.sum(text_exp, axis=1),
        jnp.dot(text_exp.astype(jnp.bfloat16), text_values, preferred_element_type=jnp.float32),
    )
    state = start_state
    piece_keys = lax.all_gather(keys_own, "tiles", axis=0, tiled=True)
    piece_values = lax.all_gather(values_own, "tiles", axis=0, tiled=True)
    piece_ids = lax.all_gather(tile_marks, "tiles", axis=0, tiled=True)
    tiles_in = piece_ids.shape[0]
    blocks = tiles_in // per_dev
    key_blocks = piece_keys.reshape(blocks, per_dev * TILE, HD)
    value_blocks = piece_values.reshape(blocks, per_dev * TILE, HD)
    id_blocks = piece_ids.reshape(blocks, per_dev)

    def step(carry, block):
        top, total, accum = carry
        block_keys, block_values, block_ids = block
        allowed = jnp.any(own_marks[:, :, None] == block_ids[None, None, :], axis=1)
        scores = jnp.dot(queries, block_keys.T, preferred_element_type=jnp.float32) * factor
        scores = scores.reshape(per_dev, TILE, per_dev, TILE)
        scores = jnp.where(allowed[:, None, :, None], scores, -jnp.inf).reshape(
            tok_rows, per_dev * TILE
        )
        new_top = jnp.maximum(top, jnp.max(scores, axis=1))
        shrink = jnp.exp(top - new_top)
        weights = jnp.exp(scores - new_top[:, None])
        accum = accum * shrink[:, None] + jnp.dot(
            weights.astype(jnp.bfloat16), block_values, preferred_element_type=jnp.float32
        )
        return ((new_top, total * shrink + jnp.sum(weights, axis=1), accum), None)

    state, unused = lax.scan(step, state, (key_blocks, value_blocks, id_blocks))
    top, total, accum = state
    attended = (accum / total[:, None]).astype(jnp.bfloat16)
    product = jnp.dot(
        lax.all_gather(attended, ("heads", "cfg"), axis=1, tiled=True),
        proj_weight,
        preferred_element_type=jnp.float32,
    )
    width_local = latents.shape[1]
    gate_slice = lax.dynamic_slice_in_dim(
        modulation[2], lax.axis_index(("heads", "cfg")) * width_local, width_local, 0
    )
    return (latents.astype(jnp.float32) + gate_slice * product).astype(jnp.bfloat16)


def solution(mesh):
    in_specs = (
        P(("groups", "tiles"), ("heads", "cfg")),
        P("groups", None),
        P(None, ("heads", "cfg")),
        P(),
        P(),
        P("groups", ("heads", "cfg")),
        P("groups"),
        P(("groups", "tiles")),
        P("groups", None),
        P(None, ("heads", "cfg")),
    )
    out_specs = P(("groups", "tiles"), ("heads", "cfg"))
    return jax.shard_map(body, mesh=mesh, in_specs=in_specs, out_specs=out_specs, check_vma=False)
```

profile of v0, /device:TPU:0, one launch (start us, length us, event | category | flops | bytes accessed | tf_op | source)
XLA Modules:
  0.0 145.6 jit_solution(16424018379306024338)
XLA Ops:
  7.3 1.2 dynamic-slice.1
  9.9 9.9 %all-reduce = s32[8]{0:T(128)S(1)} all-reduce(s32[8]{0:T(128)S(1)} %get-tuple-element.80), channel_id=1, replica_groups=mesh['groups'=2,'tiles'=4,'heads'=2,'cfg'=2] {'tiles'}, use_global_device_ids=true, to_apply=%add | all-reduce | flops 8 | bytes 64
  20.6 1.7 %copy.27 = bf16[256,256]{0,1:T(8,128)(2,1)} copy(bf16[256,256]{1,0:T(8,128)(2,1)} %param.17) | data formatting | bytes 262144 | tf_op args[5]
  22.2 1.2 gather_fusion
  25.1 24.0 %all-gather.3.cloned.1.call-done = bf16[768,3072]{1,0:T(8,128)(2,1)} async-done(((bf16[768,768]{1,0:T(8,128)(2,1)}), bf16[768,3072]{1,0:T(8,128)(2,1)}) %all-gather.3.cloned.1.call-update) | async-done | bytes 4718608 | tf_op jit(solution)/shard_map/all_gather | solution.py:34
  49.1 3.2 %convert_reduce_fusion = f32[768]{0:T(1024)S(1)} fusion(bf16[768,3072]{1,0:T(8,128)(2,1)} %all-gather.3.cloned.1.call-done), kind=kLoop, calls=%fused_computation.19 | loop fusion | flops 4717824 | bytes 4721664 | tf_op jit(solution)/shard_map/reduce_sum | solution.py:36
  52.9 1.4 fusion.13
  54.2 2.8 %fusion.17 = f32[768,384]{0,1:T(8,128)S(1)} fusion(bf16[3072,384]{1,0:T(8,128)(2,1)S(1)} %copy-done, bf16[768,3072]{1,0:T(8,128)(2,1)S(1)} %copy-done.1, f32[3072]{0:T(1024)S(1)} %bitcast.80, f32[3072]{0:T(1024)S(1)} %bitcast.81, f32[768]{0:T(1024)S(1)} %add_rsqrt_fusion.2, f32[768]{0:T(1024)S(1)} %broadcast_multiply_fusion), kind=kOutput, calls=%fused_computation.26 | convolution fusion | flops 1826095104 | bytes 8288256 | tf_op jit(solution)/shard_map/dot_general | solution.py:42
  59.3 1.3 fusion.38
  61.9 19.9 %all-gather = bf16[3072,1,128]{0,2,1:T(8,128)(2,1)} all-gather(bf16[768,1,128]{0,2,1:T(8,128)(2,1)S(1)} %slice.51), channel_id=2, replica_groups=mesh['groups'=2,'tiles'=4,'heads'=2,'cfg'=2] {'tiles'}, dimensions={0}, use_global_device_ids=true | all-gather | bytes 983040 | tf_op jit(solution)/shard_map/all_gather | solution.py:66
  81.9 2.3 %copy.31 = bf16[3072,1,128]{2,0,1:T(8,128)(2,1)} copy(bf16[3072,1,128]{0,2,1:T(8,128)(2,1)} %all-gather) | data formatting | bytes 1572864 | tf_op jit(solution)/shard_map/all_gather | solution.py:66
  85.2 18.7 %all_gather.17 = bf16[3072,128]{0,1:T(8,128)(2,1)} all-gather(bf16[768,128]{0,1:T(8,128)(2,1)S(1)} %multiply_convert_fusion), channel_id=1, replica_groups=mesh['groups'=2,'tiles'=4,'heads'=2,'cfg'=2] {'tiles'}, dimensions={0}, use_global_device_ids=true | all-gather | bytes 983040 | tf_op jit(solution)/shard_map/all_gather | solution.py:65
  103.9 2.3 %copy.30 = bf16[3072,128]{1,0:T(8,128)(2,1)} copy(bf16[3072,128]{0,1:T(8,128)(2,1)} %all_gather.17) | data formatting | bytes 1572864 | tf_op jit(solution)/shard_map/all_gather | solution.py:65
  106.2 21.4 %while.14 = (s32[]{:T(128)}, f32[768]{0:T(1024)S(1)}, f32[768]{0:T(1024)S(1)}, f32[768,128]{1,0:T(8,128)S(1)}, s32[2,27]{1,0:T(2,128)S(1)}, /*index=5*/s32[4,2]{...) while((s32[]{:T(128)}, f32[768]{0:T(1024)S(1)}, ...), condition=%wide.region_10.11_spmd, body=%wide.region_6.10_spmd.sunk | while | flops 306316992 | bytes 12042609 | solution.py:91
  108.1 1.5 %fusion.53 = (f32[768]{0:T(1024)S(1)}, f32[768,768]{0,1:T(8,128)S(1)}) fusion(pred[768,768]{0,1:T(32,128)(4,1)S(1)} %copy.37, bf16[768,128]{1,0:T(8,128)(2,1)S(1)} %get-tuple-element.174, bf16[4,768,128]{2,1,0:T(8,128)(2,1)} %get-tuple-element.173, s32[]{:T(128)S(6)} %copy.43), kind=kOutput, calls=%fused_computation.66.clone.1 | convolution fusion | flops 152763648 | bytes 3345412 | tf_op jit(solution)/shard_map/while/body/eval_jaxpr/dot_general | solution.py:78
  109.9 1.6 %convolution_add_fusion.2 = f32[768,128]{1,0:T(8,128)S(1)} fusion(f32[768,768]{0,1:T(8,128)S(1)} %get-tuple-element.144, f32[768]{0:T(1024)S(1)} %max.4, f32[768,128]{1,0:T(8,128)S(1)} %get-tuple-element.160, bf16[4,768,128]{2,1,0:T(8,128)(2,1)} %get-tuple-element.175, s32[]{:T(128)S(6)} %copy.43, f32[768]{0:T(1024)S(1)} %get-tuple-element.146), kind=kOutput, calls=%fused_computation.5.clone.1 | convolution fusion | flops 152371200 | bytes 3348484 | tf_op jit(solution)/shard_map/while/body/eval_jaxpr/dot_general | solution.py:86
  113.4 1.5 %fusion.53 = (f32[768]{0:T(1024)S(1)}, f32[768,768]{0,1:T(8,128)S(1)}) fusion(pred[768,768]{0,1:T(32,128)(4,1)S(1)} %copy.37, bf16[768,128]{1,0:T(8,128)(2,1)S(1)} %get-tuple-element.174, bf16[4,768,128]{2,1,0:T(8,128)(2,1)} %get-tuple-element.173, s32[]{:T(128)S(6)} %copy.43), kind=kOutput, calls=%fused_computation.66.clone.1 | convolution fusion | flops 152763648 | bytes 3345412 | tf_op jit(solution)/shard_map/while/body/eval_jaxpr/dot_general | solution.py:78
  115.3 1.6 %convolution_add_fusion.2 = f32[768,128]{1,0:T(8,128)S(1)} fusion(f32[768,768]{0,1:T(8,128)S(1)} %get-tuple-element.144, f32[768]{0:T(1024)S(1)} %max.4, f32[768,128]{1,0:T(8,128)S(1)} %get-tuple-element.160, bf16[4,768,128]{2,1,0:T(8,128)(2,1)} %get-tuple-element.175, s32[]{:T(128)S(6)} %copy.43, f32[768]{0:T(1024)S(1)} %get-tuple-element.146), kind=kOutput, calls=%fused_computation.5.clone.1 | convolution fusion | flops 152371200 | bytes 3348484 | tf_op jit(solution)/shard_map/while/body/eval_jaxpr/dot_general | solution.py:86
  118.8 1.5 %fusion.53 = (f32[768]{0:T(1024)S(1)}, f32[768,768]{0,1:T(8,128)S(1)}) fusion(pred[768,768]{0,1:T(32,128)(4,1)S(1)} %copy.37, bf16[768,128]{1,0:T(8,128)(2,1)S(1)} %get-tuple-element.174, bf16[4,768,128]{2,1,0:T(8,128)(2,1)} %get-tuple-element.173, s32[]{:T(128)S(6)} %copy.43), kind=kOutput, calls=%fused_computation.66.clone.1 | convolution fusion | flops 152763648 | bytes 3345412 | tf_op jit(solution)/shard_map/while/body/eval_jaxpr/dot_general | solution.py:78
  120.7 1.6 %convolution_add_fusion.2 = f32[768,128]{1,0:T(8,128)S(1)} fusion(f32[768,768]{0,1:T(8,128)S(1)} %get-tuple-element.144, f32[768]{0:T(1024)S(1)} %max.4, f32[768,128]{1,0:T(8,128)S(1)} %get-tuple-element.160, bf16[4,768,128]{2,1,0:T(8,128)(2,1)} %get-tuple-element.175, s32[]{:T(128)S(6)} %copy.43, f32[768]{0:T(1024)S(1)} %get-tuple-element.146), kind=kOutput, calls=%fused_computation.5.clone.1 | convolution fusion | flops 152371200 | bytes 3348484 | tf_op jit(solution)/shard_map/while/body/eval_jaxpr/dot_general | solution.py:86
  124.1 1.5 %fusion.53 = (f32[768]{0:T(1024)S(1)}, f32[768,768]{0,1:T(8,128)S(1)}) fusion(pred[768,768]{0,1:T(32,128)(4,1)S(1)} %copy.37, bf16[768,128]{1,0:T(8,128)(2,1)S(1)} %get-tuple-element.174, bf16[4,768,128]{2,1,0:T(8,128)(2,1)} %get-tuple-element.173, s32[]{:T(128)S(6)} %copy.43), kind=kOutput, calls=%fused_computation.66.clone.1 | convolution fusion | flops 152763648 | bytes 3345412 | tf_op jit(solution)/shard_map/while/body/eval_jaxpr/dot_general | solution.py:78
  126.0 1.6 %convolution_add_fusion.2 = f32[768,128]{1,0:T(8,128)S(1)} fusion(f32[768,768]{0,1:T(8,128)S(1)} %get-tuple-element.144, f32[768]{0:T(1024)S(1)} %max.4, f32[768,128]{1,0:T(8,128)S(1)} %get-tuple-element.160, bf16[4,768,128]{2,1,0:T(8,128)(2,1)} %get-tuple-element.175, s32[]{:T(128)S(6)} %copy.43, f32[768]{0:T(1024)S(1)} %get-tuple-element.146), kind=kOutput, calls=%fused_computation.5.clone.1 | convolution fusion | flops 152371200 | bytes 3348484 | tf_op jit(solution)/shard_map/while/body/eval_jaxpr/dot_general | solution.py:86
  127.8 7.7 %all_gather.19 = bf16[768,512]{1,0:T(8,128)(2,1)S(1)} all-gather(bf16[768,128]{1,0:T(8,128)(2,1)S(1)} %divide_convert_fusion), channel_id=1, replica_groups=mesh['groups'=2,'tiles'=4,'heads'=2,'cfg'=2] {'heads','cfg'}, dimensions={1}, use_global_device_ids=true | all-gather | bytes 983040 | tf_op jit(solution)/shard_map/all_gather | solution.py:95
  135.5 3.3 %add_convert_fusion = bf16[768,768]{1,0:T(8,128)(2,1)} fusion(bf16[768,768]{1,0:T(8,128)(2,1)} %param.12, bf16[768,512]{1,0:T(8,128)(2,1)S(1)} %all_gather.19, bf16[512,768]{1,0:T(8,128)(2,1)} %param.21, f32[768]{0:T(1024)S(1)} %dynamic-slice_reduce_fusion), kind=kOutput, calls=%fused_computation.31 | convolution fusion | flops 606339072 | bytes 3935232 | tf_op jit(solution)/shard_map/dot_general | solution.py:94
  (68 shorter events, 17.4 us)
Async XLA Ops:
  6.5 47.7 %copy-start = (bf16[3072,384]{1,0:T(8,128)(2,1)S(1)}, bf16[3072,384]{1,0:T(8,128)(2,1)}, u32[]{:S(2)}) copy-start(bf16[3072,384]{1,0:T(8,128)(2,1)} %param.14) | copy-start | bytes 7077892
  6.5 42.6 %all-gather.3.cloned.1.call-start = ((), (), s32[]{:S(2)}) async-start(), calls=%async_computation | async-start | bytes 5898240 | tf_op jit(solution)/shard_map/all_gather | solution.py:34
  49.1 3.8 %copy-start.1 = (bf16[768,3072]{1,0:T(8,128)(2,1)S(1)}, bf16[768,3072]{1,0:T(8,128)(2,1)}, u32[]{:S(2)}) copy-start(bf16[768,3072]{1,0:T(8,128)(2,1)} %all-gather.3.cloned.1.call-done) | copy-start | bytes 14155780
  57.1 1.0 copy-start.2
  60.6 23.6 %copy-start.3 = (f32[128]{0:T(128)S(1)}, f32[128]{0:T(128)}, u32[]{:S(2)}) copy-start(f32[128]{0:T(128)} %param.16) | copy-start | bytes 1540
Sparse Core Ops, SparseCore 0:
  8.9 40.1 all-gather.2
where the time goes:
time: 146 us
  blocking collectives  56.2 us (38%)
  waiting for transfers between devices  24.8 us (17%)
  matrix products  20.7 us (14%)
  local copies, waits for them, and re-layouts  17.2 us (12%)
  between operations  14.9 us (10%)
  other arithmetic  11.6 us (8%)
    all_gather x1, waiting for transfers between devices, body(): gathered = lax.all_gather(latents, ('heads', 'cfg'), axis=1, tiled=True)  24 us
    all_gather x1, blocking collectives, body(): piece_values = lax.all_gather(values_own, 'tiles', axis=0, tiled=True)  19.9 us
    all_gather x1, blocking collectives, body(): piece_keys = lax.all_gather(keys_own, 'tiles', axis=0, tiled=True)  18.7 us
    unnamed x1, blocking collectives  9.89 us
    all_gather x1, blocking collectives, body(): lax.all_gather(attended, ('heads', 'cfg'), axis=1, tiled=True)  7.7 us
    dot_general x4, matrix products, step(): jnp.dot(weights.astype(jnp.bfloat16), block_values, preferred_element_typ...  6.24 us
    dot_general x4, matrix products, step(): jnp.dot(queries, block_keys.T, preferred_element_type=jnp.float32) * factor  5.95 us
    broadcast_in_dim x8, local copies, waits for them, and re-layouts, step(): jnp.where(allowed[:, None, :, None], scores, -jnp.inf)  5.45 us
  transfers between devices with their start and end apart: 1, of which 1 were waited for; matrix products, arithmetic and copies ran while one was open for 5% of the time, Pallas kernels for 0%

commit v1 on v0

v1 whole, which is shorter than its diff:
```python
import functools
import math

import jax
import jax.numpy as jnp
from jax import lax
from jax.experimental import pallas as pl
from jax.experimental.pallas import tpu as pltpu
from jax.sharding import PartitionSpec as P

HD = 128
TILE = 384
TXT = 256
CHUNKS = ((0, 256), (256, 256), (512, 128), (640, 128))

epsilon = 1e-06
LOG2E = math.log2(math.e)
FACTOR = LOG2E / math.sqrt(HD)

SMEM = pl.BlockSpec(memory_space=pltpu.SMEM)
VMEM = pl.BlockSpec(memory_space=pltpu.VMEM)
NT = (((1,), (1,)), ((), ()))


def rms_norm(values, gain):
    return values * lax.rsqrt(jnp.mean(values * values, axis=-1, keepdims=True) + epsilon) * gain


def project_kernel(count, place_ref, *refs):
    pieces = refs[:count]
    modulation_ref, weight_ref, query_gain_ref, key_gain_ref, query_ref, kv_ref = refs[count:]
    width = pieces[0].shape[1]
    features = width * count
    total = sum(jnp.sum(piece[...].astype(jnp.float32), axis=1, keepdims=True) for piece in pieces)
    average = total / features
    spread = 0.0
    for piece in pieces:
        centred = piece[...].astype(jnp.float32) - average
        spread = spread + jnp.sum(centred * centred, axis=1, keepdims=True)
    scale = lax.rsqrt(spread / features + epsilon)
    projected = 0.0
    for place, piece in enumerate(pieces):
        first = place_ref[place] * width
        if count > 1:
            first = pl.multiple_of(first, width)
        span = pl.ds(first, width)
        centred = piece[...].astype(jnp.float32) - average
        modulated = (
            centred * scale * (1.0 + modulation_ref[1:2, span]) + modulation_ref[0:1, span]
        ).astype(jnp.bfloat16)
        projected = projected + jnp.dot(
            modulated, weight_ref[span, :], preferred_element_type=jnp.float32
        )
    query_ref[...] = rms_norm(projected[:, :HD], query_gain_ref[...]).astype(jnp.bfloat16)
    kv_ref[:, :HD] = rms_norm(projected[:, HD : 2 * HD], key_gain_ref[...]).astype(jnp.bfloat16)
    kv_ref[:, HD:] = projected[:, 2 * HD :].astype(jnp.bfloat16)


def project(places, pieces, blocks, modulation, weight, query_gain, key_gain, rows):
    count = len(pieces)
    specs = [pl.BlockSpec((rows, piece.shape[1]), lambda i, block=block: (block, 0)) for piece, block in zip(pieces, blocks)]
    return pl.pallas_call(
        functools.partial(project_kernel, count),
        grid=(1,),
        out_shape=(
            jax.ShapeDtypeStruct((rows, HD), jnp.bfloat16),
            jax.ShapeDtypeStruct((rows, 2 * HD), jnp.bfloat16),
        ),
        in_specs=[SMEM] + specs + [VMEM] * 4,
        out_specs=(VMEM, VMEM),
        compiler_params=pltpu.CompilerParams(vmem_limit_bytes=32 * 2**20),
        cost_estimate=pl.CostEstimate(
            flops=2 * rows * 3072 * 384, bytes_accessed=rows * 6144 + 2 * 3072 * 384, transcendentals=rows
        ),
    )(places, *pieces, modulation, weight, query_gain, key_gain)


def attend_block(query, shift, keys, values):
    scores = lax.dot_general(query, keys, NT, preferred_element_type=jnp.float32)
    strips = [
        jnp.exp2(scores[:, at : at + HD] * FACTOR - shift) for at in range(0, keys.shape[0], HD)
    ]
    weights = jnp.concatenate(strips, axis=1) if len(strips) > 1 else strips[0]
    product = jnp.dot(weights.astype(jnp.bfloat16), values, preferred_element_type=jnp.float32)
    return sum(strips), product


def segments(start, size):
    out = []
    at = start
    while at < start + size:
        end = min(start + size, (at // TILE + 1) * TILE)
        out.append((at - start, end - at, at // TILE))
        at = end
    return out


def attend_kernel(plan, tiles, first, last, stacked, allow_ref, *refs):
    refs = list(refs)
    queries = [refs.pop(0) for _ in CHUNKS]
    kvs = [refs.pop(0) for _ in plan]
    if first:
        length_ref, text_ref, query_gain_ref, key_gain_ref = [refs.pop(0) for _ in range(4)]
    else:
        shift_in, total_in, accum_in = [refs.pop(0) for _ in range(3)]
    if last:
        out_ref = refs.pop(0)
        total_ref, accum_ref, query_ref = refs
        shift_ref = shift_in
    else:
        shift_ref, total_ref, accum_ref, query_ref = refs
    for (start, size), piece in zip(CHUNKS, queries):
        query_ref[start : start + size, :] = piece[...]
    if first:
        bound = (
            jnp.max(jnp.abs(query_gain_ref[...])) * jnp.max(jnp.abs(key_gain_ref[...])) * (1.02 * HD * FACTOR)
        )
        live = lax.broadcasted_iota(jnp.int32, (TILE, TXT), 1) < length_ref[0]
    for tile in range(tiles):
        rows = slice(tile * TILE, (tile + 1) * TILE)
        if first:
            scores = lax.dot_general(query_ref[rows, :], text_ref[:, :HD], NT, preferred_element_type=jnp.float32)
            scores = jnp.where(live, scores * FACTOR, -jnp.inf)
            top = jnp.maximum(jnp.max(scores, axis=1, keepdims=True), bound)
            weights = jnp.exp2(scores - top)
            shift_ref[rows, :] = jnp.broadcast_to(top, (TILE, HD))
            total_ref[rows, :] = weights[:, :HD] + weights[:, HD:]
            accum_ref[rows, :] = jnp.dot(
                weights.astype(jnp.bfloat16), text_ref[:, HD:], preferred_element_type=jnp.float32
            )
        else:
            if not last:
                shift_ref[rows, :] = shift_in[rows, :]
            total_ref[rows, :] = total_in[rows, :]
            accum_ref[rows, :] = accum_in[rows, :]
        for (source, start, size), kv in zip(plan, kvs):
            for at, length, slot in segments(start, size):

                def work(source, keys, values, rows=rows, tile=tile, slot=slot):
                    @pl.when(allow_ref[tile, source * tiles + slot] > 0)
                    def _():
                        total, product = attend_block(query_ref[rows, :], shift_ref[rows, :], keys(), values())
                        total_ref[rows, :] += total
                        accum_ref[rows, :] += product

                span = slice(at, at + length)
                if stacked:

                    def step(source, carry, kv=kv, span=span, work=work):
                        work(source, lambda: kv[source, span, :HD], lambda: kv[source, span, HD:])
                        return carry

                    lax.fori_loop(0, kv.shape[0], step, 0)
                else:
                    work(source, lambda: kv[span, :HD], lambda: kv[span, HD:])
        if last:
            total = jnp.sum(total_ref[rows, :], axis=1, keepdims=True)
            out_ref[rows, :] = (accum_ref[rows, :] / total).astype(jnp.bfloat16)


def attend(plan, kvs, allow, queries, tiles, start=None, state=None, last=False, stacked=False):
    rows = tiles * TILE
    first = state is None
    extra = start if first else state
    part = jax.ShapeDtypeStruct((rows, HD), jnp.float32)
    scratch = [pltpu.VMEM((rows, HD), jnp.bfloat16)]
    if last:
        out_shape = jax.ShapeDtypeStruct((rows, HD), jnp.bfloat16)
        scratch = [pltpu.VMEM((rows, HD), jnp.float32)] * 2 + scratch
    else:
        out_shape = (part,) * 3
    keys = sum(kv.size // (2 * HD) for kv in kvs) + (TXT if first else 0)
    return pl.pallas_call(
        functools.partial(attend_kernel, plan, tiles, first, last, stacked),
        out_shape=out_shape,
        in_specs=[SMEM] + [VMEM] * (len(queries) + len(kvs)) + ([SMEM] if first else []) + [VMEM] * 3,
        out_specs=VMEM if last else (VMEM,) * 3,
        scratch_shapes=scratch,
        compiler_params=pltpu.CompilerParams(vmem_limit_bytes=32 * 2**20),
        cost_estimate=pl.CostEstimate(
            flops=4 * rows * keys * HD, bytes_accessed=rows * HD * 14 + keys * HD * 4, transcendentals=rows * keys
        ),
    )(allow, *queries, *kvs, *extra)


def merge_kernel(count, place_ref, *refs):
    pieces = refs[:count]
    weight_ref, latents_ref, gate_ref, out_ref = refs[count:]
    depth = pieces[0].shape[1]
    product = 0.0
    for place, piece in enumerate(pieces):
        first = place_ref[place] * depth
        if count > 1:
            first = pl.multiple_of(first, depth)
        product = product + jnp.dot(
            piece[...], weight_ref[pl.ds(first, depth), :], preferred_element_type=jnp.float32
        )
    out_ref[...] = (latents_ref[...].astype(jnp.float32) + gate_ref[...] * product).astype(jnp.bfloat16)


def merge(places, pieces, weight, latents, gate):
    rows, width = latents.shape
    block = 256
    return pl.pallas_call(
        functools.partial(merge_kernel, len(pieces)),
        grid=(rows // block,),
        out_shape=jax.ShapeDtypeStruct((rows, width), jnp.bfloat16),
        in_specs=[SMEM]
        + [pl.BlockSpec((block, piece.shape[1]), lambda i: (i, 0)) for piece in pieces]
        + [
            pl.BlockSpec(weight.shape, lambda i: (0, 0)),
            pl.BlockSpec((block, width), lambda i: (i, 0)),
            pl.BlockSpec(gate.shape, lambda i: (0, 0)),
        ],
        out_specs=pl.BlockSpec((block, width), lambda i: (i, 0)),
        compiler_params=pltpu.CompilerParams(vmem_limit_bytes=32 * 2**20),
        cost_estimate=pl.CostEstimate(
            flops=2 * rows * width * weight.shape[0],
            bytes_accessed=rows * width * 4 + weight.size * 2 + rows * weight.shape[0] * 2,
            transcendentals=0,
        ),
    )(places, *pieces, weight, latents, gate)


def shifted(values, axis, size, by):
    return lax.ppermute(values, axis, [(at, (at + by) % size) for at in range(size)])


def body(
    heads_size,
    cfg_size,
    tiles_size,
    latents,
    modulation,
    qkv_weight,
    query_gain,
    key_gain,
    text_kv,
    text_len,
    tile_ids,
    windows,
    proj_weight,
):
    pairs = heads_size == 2 and cfg_size == 2
    stacked = tiles_size > 4
    per_dev = tile_ids.shape[0]
    width = latents.shape[1]
    me = lax.axis_index(("heads", "cfg"))
    query_gain = query_gain[None, :]
    key_gain = key_gain[None, :]

    if pairs:
        across = [shifted(latents[start : start + size], "heads", 2, 1) for start, size in CHUNKS]
        beside = shifted(latents, "cfg", 2, 1)
        places = jnp.stack([me, me ^ 1, me ^ 2, me ^ 3]).astype(jnp.int32)
    else:
        gathered = lax.all_gather(latents, ("heads", "cfg"), axis=1, tiled=True)
        places = jnp.zeros((1,), jnp.int32)

    if stacked:
        ids = lax.all_gather(tile_ids, "tiles", axis=0, tiled=True)
    else:
        ids = jnp.concatenate([tile_ids] + [shifted(tile_ids, "tiles", tiles_size, by) for by in range(1, tiles_size)])
    allow = jnp.any(windows[tile_ids][:, :, None] == ids[None, None, :], axis=1).astype(jnp.int32)

    queries = []
    kvs = []
    remote = []
    for number, (start, size) in enumerate(CHUNKS):
        block = start // size
        if pairs:
            far = across[number]
            pieces = [latents, beside, far, shifted(far, "cfg", 2, 1)]
            blocks = [block, block, 0, 0]
        else:
            pieces = [gathered]
            blocks = [block]
        query, kv = project(places, pieces, blocks, modulation, qkv_weight, query_gain, key_gain, size)
        queries.append(query)
        kvs.append(kv)
        if stacked:
            remote.append([lax.all_gather(kv, "tiles", axis=0)])
        else:
            remote.append([shifted(kv, "tiles", tiles_size, by) for by in range(1, tiles_size)])

    begin = (text_len, text_kv, query_gain, key_gain)

    def plan_of(numbers):
        plan, arrays = [], []
        for number in numbers:
            for by, array in enumerate(remote[number]):
                plan.append((by + 1,) + CHUNKS[number])
                arrays.append(array)
        return plan, arrays

    own_plan, own = ([], []) if stacked else ([(0,) + chunk for chunk in CHUNKS], kvs)
    state = attend(own_plan, own, allow, queries, per_dev, start=begin)
    final = len(CHUNKS) - 1
    plan, arrays = plan_of(range(final - 1))
    state = attend(plan, arrays, allow, queries, per_dev, state=state, stacked=stacked)
    plan, arrays = plan_of([final - 1])
    state = attend(plan, arrays, allow, queries, per_dev, state=state, stacked=stacked)
    plan, arrays = plan_of([final])
    attended = attend(plan, arrays, allow, queries, per_dev, state=state, last=True, stacked=stacked)

    if pairs:
        far = shifted(attended, "heads", 2, 1)
        pieces = [attended, shifted(attended, "cfg", 2, 1), far, shifted(far, "cfg", 2, 1)]
    else:
        pieces = [lax.all_gather(attended, ("heads", "cfg"), axis=1, tiled=True)]
    gate = lax.dynamic_slice_in_dim(modulation[2:3], me * width, width, 1)
    return merge(places, pieces, proj_weight, latents, gate)


def solution(mesh):
    in_specs = (
        P(("groups", "tiles"), ("heads", "cfg")),
        P("groups", None),
        P(None, ("heads", "cfg")),
        P(),
        P(),
        P("groups", ("heads", "cfg")),
        P("groups"),
        P(("groups", "tiles")),
        P("groups", None),
        P(None, ("heads", "cfg")),
    )
    out_specs = P(("groups", "tiles"), ("heads", "cfg"))
    run = functools.partial(body, mesh.shape["heads"], mesh.shape["cfg"], mesh.shape["tiles"])
    return jax.shard_map(run, mesh=mesh, in_specs=in_specs, out_specs=out_specs, check_vma=False)
```

time: 146 us -> 95.6 us (0.65)
  blocking collectives: 56.2 us -> 0 us
  starting transfers between devices: 0.01 us -> 35.7 us
  Pallas kernels: 0 us -> 26.4 us
  matrix products: 20.7 us -> 0 us
  between operations: 14.9 us -> 0.89 us
  local copies, waits for them, and re-layouts: 17.2 us -> 4.2 us
  other arithmetic: 11.6 us -> 0.35 us
  waiting for transfers between devices: 24.8 us -> 27.5 us
    all_gather x3 -> x0, blocking collectives: 46.3 us -> none  [the longest x1 19.9 us: body(): piece_values = lax.all_gather(values_own, 'tiles', axis=0, tiled=True)]
    ppermute x0 -> x27, starting transfers between devices: none -> 35.7 us  [shifted(): lax.ppermute(values, axis, [(at, (at + by) % size) for at in range(size)])]
    ppermute x0 -> x27, waiting for transfers between devices: none -> 27.5 us  [shifted(): lax.ppermute(values, axis, [(at, (at + by) % size) for at in range(size)])]
    pallas_call x0 -> x9, Pallas kernels: none -> 26.4 us  [the longest x4 13.8 us: attend(): pl.pallas_call(functools.partial(attend_kernel, plan, tiles, first, last,...]
    all_gather x1 -> x0, waiting for transfers between devices: 24 us -> none  [body(): gathered = lax.all_gather(latents, ('heads', 'cfg'), axis=1, tiled=True)]
    dot_general x12 -> x0, matrix products: 20.7 us -> none  [the longest x4 6.24 us: step(): jnp.dot(weights.astype(jnp.bfloat16), block_values, preferred_element_typ...]
    unnamed x1 -> x0, blocking collectives: 9.89 us -> none
    reduce_sum x9 -> x0, other arithmetic: 6.37 us -> none  [the longest x1 3.17 us: body(): average = jnp.mean(rows, axis=-1, keepdims=True)]
  transfers between devices with their start and end apart: 1 -> 27, of which waited for: 1 -> 6; matrix products, arithmetic and copies ran while one was open for 5% -> 3% of each run, Pallas kernels for 0% -> 22%
where the time goes in v1:
time: 95.6 us; the launch traced here: 95 us
  starting transfers between devices  35.7 us (37%)
  waiting for transfers between devices  27.5 us (29%)
  Pallas kernels  26.4 us (28%)
  local copies, waits for them, and re-layouts  4.2 us (4%)
    ppermute x27, starting transfers between devices, shifted(): lax.ppermute(values, axis, [(at, (at + by) % size) for at in range(size)])  35.7 us
    ppermute x27, waiting for transfers between devices, shifted(): lax.ppermute(values, axis, [(at, (at + by) % size) for at in range(size)])  27.5 us
    pallas_call x4, Pallas kernels, attend(): pl.pallas_call(functools.partial(attend_kernel, plan, tiles, first, last,...  13.8 us
    pallas_call x4, Pallas kernels, project(): pl.pallas_call(functools.partial(project_kernel, count), grid=(1,), out_s...  9.39 us
    pallas_call x1, Pallas kernels, merge(): pl.pallas_call(functools.partial(merge_kernel, len(pieces)), grid=(rows /...  3.17 us
    slice x2, local copies, waits for them, and re-layouts, body(): latents[start:start + size]  1.92 us
  transfers between devices with their start and end apart: 27, of which 6 were waited for; matrix products, arithmetic and copies ran while one was open for 3% of the time, Pallas kernels for 22%

profile of v1, /device:TPU:0, one launch (start us, length us, event | category | flops | bytes accessed | tf_op | source)
XLA Modules:
  0.0 95.0 jit_solution(5767897795171756195)
XLA Ops:
  1.8 2.6 %collective-permute-start.6 = (bf16[256,768]{1,0:T(8,128)(2,1)S(1)}, bf16[256,768]{1,0:T(8,128)(2,1)}, u32[]{:S(2)}, u32[]{:S(2)}) collective-permute-start(bf16[256,768]{1,0:T(8,128)(2,1)S(1)} %get-tuple-element.41), channel_id=1, source_target_pairs={{0,2},{2,0},{1,3},{3,1},{4,6},{6,4},{5,7},{7,5},{8,10},{10,8},{9,1... | collective-permute-start | bytes 1179656 | tf_op jit(solution)/shard_map/ppermute | solution.py:226
  5.2 1.9 %collective-permute-start.8 = (bf16[128,768]{1,0:T(8,128)(2,1)S(1)}, bf16[128,768]{1,0:T(8,128)(2,1)}, u32[]{:S(2)}, u32[]{:S(2)}) collective-permute-start(bf16[128,768]{1,0:T(8,128)(2,1)S(1)} %get-tuple-element.40), channel_id=1, source_target_pairs={{0,2},{2,0},{1,3},{3,1},{4,6},{6,4},{5,7},{7,5},{8,10},{10,8},{9,1... | collective-permute-start | bytes 589832 | tf_op jit(solution)/shard_map/ppermute | solution.py:226
  7.2 7.3 %collective-permute-done.6.refs_2_ = bf16[256,768]{1,0:T(8,128)(2,1)} collective-permute-done((bf16[256,768]{1,0:T(8,128)(2,1)S(1)}, bf16[256,768]{1,0:T(8,128)(2,1)}, u32[]{:S(2)}, u32[]{:S(2)}) %collective-permute-start.6) | collective-permute-done | bytes 393248 | tf_op jit(solution)/shard_map/ppermute | solution.py:226
  14.5 12.6 %collective-permute-done.8.refs_2_ = bf16[128,768]{1,0:T(8,128)(2,1)} collective-permute-done((bf16[128,768]{1,0:T(8,128)(2,1)S(1)}, bf16[128,768]{1,0:T(8,128)(2,1)}, u32[]{:S(2)}, u32[]{:S(2)}) %collective-permute-start.8) | collective-permute-done | bytes 196640 | tf_op jit(solution)/shard_map/ppermute | solution.py:226
  28.9 2.0 %collective-permute-start = (s32[2]{0:T(128)S(1)}, s32[2]{0:T(128)S(1)}, u32[]{:S(2)}, u32[]{:S(2)}) collective-permute-start(s32[2]{0:T(128)S(1)} %copy-done.9), channel_id=1, source_target_pairs={{0,4},{4,8},{8,12},{12,0},{1,5},{5,9},{9,13},{13,1},{2,6},{6,10},{... | collective-permute-start | bytes 32 | tf_op jit(solution)/shard_map/ppermute | solution.py:226
  30.9 2.6 %collective-permute-start.1 = (s32[2]{0:T(128)S(1)}, s32[2]{0:T(128)S(1)}, u32[]{:S(2)}, u32[]{:S(2)}) collective-permute-start(s32[2]{0:T(128)S(1)} %copy-done.9), channel_id=1, source_target_pairs={{0,8},{4,12},{8,0},{12,4},{1,9},{5,13},{9,1},{13,5},{2,10},{6,14},... | collective-permute-start | bytes 32 | tf_op jit(solution)/shard_map/ppermute | solution.py:226
  33.6 1.7 %copy-done.2 = bf16[3072,384]{1,0:T(8,128)(2,1)S(1)} copy-done((bf16[3072,384]{1,0:T(8,128)(2,1)S(1)}, bf16[3072,384]{1,0:T(8,128)(2,1)}, u32[]{:S(2)}) %copy-start.2) | copy-done | bytes 2359320
  35.2 3.0 %shard_map.101 = (bf16[256,128]{1,0:T(8,128)(2,1)S(1)}, bf16[256,256]{1,0:T(8,128)(2,1)S(1)}) custom-call(s32[4]{0:T(128)S(1)} %pad_add_fusion.place_ref, bf16[768,768]{1,0:T(8,128)(2,1)S(1)} %copy-done.1, bf16[768,768]{1,0:T(8,128)(2,1)S(1)} %collective-permute-done.3.refs_1_, bf16[256,768]{1,0:T(8,128)(2,1)} %collective-permute-done.6.refs_2_, ...), custom_call_target="tpu_custom_call" | custom-call | flops 603979776 | bytes 3932160 | tf_op jit(solution)/shard_map/pallas_call | solution.py:62
  39.7 2.3 %shard_map.102 = (bf16[128,128]{1,0:T(8,128)(2,1)S(1)}, bf16[128,256]{1,0:T(8,128)(2,1)S(1)}) custom-call(s32[4]{0:T(128)S(1)} %pad_add_fusion.place_ref, bf16[768,768]{1,0:T(8,128)(2,1)S(1)} %copy-done.1, bf16[768,768]{1,0:T(8,128)(2,1)S(1)} %collective-permute-done.3.refs_1_, bf16[128,768]{1,0:T(8,128)(2,1)} %collective-permute-done.8.refs_2_, ...), custom_call_target="tpu_custom_call" | custom-call | flops 301989888 | bytes 3145728 | tf_op jit(solution)/shard_map/pallas_call | solution.py:62
  42.9 3.6 %collective-permute-start.22 = (bf16[256,256]{1,0:T(8,128)(2,1)S(1)}, bf16[256,256]{1,0:T(8,128)(2,1)S(1)}, u32[]{:S(2)}, u32[]{:S(2)}) collective-permute-start(bf16[256,256]{1,0:T(8,128)(2,1)S(1)} %get-tuple-element.29.refs_5_), channel_id=1, source_target_pairs={{0,8},{4,12},{8,0},{12,4},{1,9},{5,13},{9,1},{13,5},{2,10},{6,14},... | collective-permute-start | bytes 393224 | tf_op jit(solution)/shard_map/ppermute | solution.py:226
  46.7 2.4 %shard_map.100 = (bf16[256,128]{1,0:T(8,128)(2,1)S(1)}, bf16[256,256]{1,0:T(8,128)(2,1)S(1)}) custom-call(s32[4]{0:T(128)S(1)} %pad_add_fusion.place_ref, bf16[768,768]{1,0:T(8,128)(2,1)S(1)} %copy-done.1, bf16[768,768]{1,0:T(8,128)(2,1)S(1)} %collective-permute-done.3.refs_1_, bf16[256,768]{1,0:T(8,128)(2,1)S(1)} %collective-permute-done.4.refs_2_, ...), custom_call_target="tpu_custom_call" | custom-call | flops 603979776 | bytes 3932160 | tf_op jit(solution)/shard_map/pallas_call | solution.py:62
  49.1 1.9 %collective-permute-start.18 = (bf16[256,256]{1,0:T(8,128)(2,1)S(1)}, bf16[256,256]{1,0:T(8,128)(2,1)S(1)}, u32[]{:S(2)}, u32[]{:S(2)}) collective-permute-start(bf16[256,256]{1,0:T(8,128)(2,1)S(1)} %get-tuple-element.28.refs_4_), channel_id=1, source_target_pairs={{0,4},{4,8},{8,12},{12,0},{1,5},{5,9},{9,13},{13,1},{2,6},{6,10},{... | collective-permute-start | bytes 393224 | tf_op jit(solution)/shard_map/ppermute | solution.py:226
  51.7 2.4 %collective-permute-start.20 = (bf16[256,256]{1,0:T(8,128)(2,1)S(1)}, bf16[256,256]{1,0:T(8,128)(2,1)S(1)}, u32[]{:S(2)}, u32[]{:S(2)}) collective-permute-start(bf16[256,256]{1,0:T(8,128)(2,1)S(1)} %get-tuple-element.28.refs_4_), channel_id=1, source_target_pairs={{0,12},{4,0},{8,4},{12,8},{1,13},{5,1},{9,5},{13,9},{2,14},{6,2},{... | collective-permute-start | bytes 393224 | tf_op jit(solution)/shard_map/ppermute | solution.py:226
  54.3 1.7 %shard_map.103 = (bf16[128,128]{1,0:T(8,128)(2,1)S(1)}, bf16[128,256]{1,0:T(8,128)(2,1)S(1)}) custom-call(s32[4]{0:T(128)S(1)} %pad_add_fusion.place_ref, bf16[768,768]{1,0:T(8,128)(2,1)S(1)} %copy-done.1, bf16[768,768]{1,0:T(8,128)(2,1)S(1)} %collective-permute-done.3.refs_1_, bf16[128,768]{1,0:T(8,128)(2,1)S(1)} %collective-permute-done.10.refs_2_, ...), custom_call_target="tpu_custom_call" | custom-call | flops 301989888 | bytes 3145728 | tf_op jit(solution)/shard_map/pallas_call | solution.py:62
  57.3 2.3 %collective-permute-start.17 = (bf16[128,256]{1,0:T(8,128)(2,1)S(1)}, bf16[128,256]{1,0:T(8,128)(2,1)S(1)}, u32[]{:S(2)}, u32[]{:S(2)}) collective-permute-start(bf16[128,256]{1,0:T(8,128)(2,1)S(1)} %get-tuple-element.27.refs_6_), channel_id=1, source_target_pairs={{0,12},{4,0},{8,4},{12,8},{1,13},{5,1},{9,5},{13,9},{2,14},{6,2},{... | collective-permute-start | bytes 196616 | tf_op jit(solution)/shard_map/ppermute | solution.py:226
  59.6 4.7 %shard_map.104 = (f32[768,128]{1,0:T(8,128)S(1)}, f32[768,128]{1,0:T(8,128)S(1)}, f32[768,128]{1,0:T(8,128)S(1)}) custom-call(s32[2,8]{1,0:T(2,128)S(1)} %convert_element_type.3.allow_ref, bf16[256,128]{1,0:T(8,128)(2,1)S(1)} %get-tuple-element.22.refs_0_, bf16[256,128]{1,0:T(8,128)(2,1)S(1)} %get-tuple-element.23.refs_1_, ...), custom_call_target="tpu_custom_call" | custom-call | flops 402653184 | bytes 1900544 | tf_op jit(solution)/shard_map/pallas_call | solution.py:173
  64.3 6.7 %collective-permute-start.12 = (bf16[128,256]{1,0:T(8,128)(2,1)S(1)}, bf16[128,256]{1,0:T(8,128)(2,1)S(1)}, u32[]{:S(2)}, u32[]{:S(2)}) collective-permute-start(bf16[128,256]{1,0:T(8,128)(2,1)S(1)} %get-tuple-element.26.refs_7_), channel_id=1, source_target_pairs={{0,4},{4,8},{8,12},{12,0},{1,5},{5,9},{9,13},{13,1},{2,6},{6,10},{... | collective-permute-start | bytes 196616 | tf_op jit(solution)/shard_map/ppermute | solution.py:226
  72.6 2.8 %collective-permute-start.14 = (bf16[128,256]{1,0:T(8,128)(2,1)S(1)}, bf16[128,256]{1,0:T(8,128)(2,1)S(1)}, u32[]{:S(2)}, u32[]{:S(2)}) collective-permute-start(bf16[128,256]{1,0:T(8,128)(2,1)S(1)} %get-tuple-element.26.refs_7_), channel_id=1, source_target_pairs={{0,12},{4,0},{8,4},{12,8},{1,13},{5,1},{9,5},{13,9},{2,14},{6,2},{... | collective-permute-start | bytes 196616 | tf_op jit(solution)/shard_map/ppermute | solution.py:226
  75.5 5.0 %shard_map.105 = (f32[768,128]{1,0:T(8,128)S(1)}, f32[768,128]{1,0:T(8,128)S(1)}, f32[768,128]{1,0:T(8,128)S(1)}) custom-call(s32[2,8]{1,0:T(2,128)S(1)} %convert_element_type.3.allow_ref, bf16[256,128]{1,0:T(8,128)(2,1)S(1)} %get-tuple-element.22.refs_0_, bf16[256,128]{1,0:T(8,128)(2,1)S(1)} %get-tuple-element.23.refs_1_, ...), custom_call_target="tpu_custom_call" | custom-call | flops 603979776 | bytes 2162688 | tf_op jit(solution)/shard_map/pallas_call | solution.py:173
  80.5 1.9 %shard_map.106 = (f32[768,128]{1,0:T(8,128)S(1)}, f32[768,128]{1,0:T(8,128)S(1)}, f32[768,128]{1,0:T(8,128)S(1)}) custom-call(s32[2,8]{1,0:T(2,128)S(1)} %convert_element_type.3.allow_ref, bf16[256,128]{1,0:T(8,128)(2,1)S(1)} %get-tuple-element.22.refs_0_, bf16[256,128]{1,0:T(8,128)(2,1)S(1)} %get-tuple-element.23.refs_1_, ...), custom_call_target="tpu_custom_call" | custom-call | flops 150994944 | bytes 1572864 | tf_op jit(solution)/shard_map/pallas_call | solution.py:173
  82.5 2.2 %shard_map.107.refs_0_ = bf16[768,128]{1,0:T(8,128)(2,1)S(1)} custom-call(s32[2,8]{1,0:T(2,128)S(1)} %convert_element_type.3.allow_ref, bf16[256,128]{1,0:T(8,128)(2,1)S(1)} %get-tuple-element.22.refs_0_, bf16[256,128]{1,0:T(8,128)(2,1)S(1)} %get-tuple-element.23.refs_1_, bf16[128,128]{1,0:T(8,128)(2,1)S(1)} %get-tuple-element.24.refs_2_, ...), custom_call_target="tpu_custom_call" | custom-call | flops 150994944 | bytes 1572864 | tf_op jit(solution)/shard_map/pallas_call | solution.py:173
  84.6 1.6 %collective-permute-start.25 = (bf16[768,128]{1,0:T(8,128)(2,1)S(1)}, bf16[768,128]{1,0:T(8,128)(2,1)S(1)}, u32[]{:S(2)}, u32[]{:S(2)}) collective-permute-start(bf16[768,128]{1,0:T(8,128)(2,1)S(1)} %shard_map.107.refs_0_), channel_id=1, source_target_pairs={{0,2},{2,0},{1,3},{3,1},{4,6},{6,4},{5,7},{7,5},{8,10},{10,8},{9,1... | collective-permute-start | bytes 589832 | tf_op jit(solution)/shard_map/ppermute | solution.py:226
  86.2 4.2 %collective-permute-done.25.refs_2_ = bf16[768,128]{1,0:T(8,128)(2,1)S(1)} collective-permute-done((bf16[768,128]{1,0:T(8,128)(2,1)S(1)}, bf16[768,128]{1,0:T(8,128)(2,1)S(1)}, u32[]{:S(2)}, u32[]{:S(2)}) %collective-permute-start.25) | collective-permute-done | bytes 196640 | tf_op jit(solution)/shard_map/ppermute | solution.py:226
  91.8 3.2 %shard_map.108 = bf16[768,768]{1,0:T(8,128)(2,1)} custom-call(s32[4]{0:T(128)S(1)} %pad_add_fusion.place_ref, bf16[768,128]{1,0:T(8,128)(2,1)S(1)} %shard_map.107.refs_0_, bf16[768,128]{1,0:T(8,128)(2,1)S(1)} %collective-permute-done.24.refs_1_, bf16[768,128]{1,0:T(8,128)(2,1)S(1)} %collective-permute-done.25.refs_2_, ...), custom_call_target="tpu_custom_call" | custom-call | flops 603979776 | bytes 3932160 | tf_op jit(solution)/shard_map/pallas_call | solution.py:204
  (70 shorter events, 11.5 us)
Async XLA Ops:
  0.0 30.9 %collective-permute-start.3 = (bf16[768,768]{1,0:T(8,128)(2,1)}, bf16[768,768]{1,0:T(8,128)(2,1)S(1)}, u32[]{:S(2)}, u32[]{:S(2)}) collective-permute-start(bf16[768,768]{1,0:T(8,128)(2,1)} %refs_5_.9), channel_id=1, source_target_pairs={{0,1},{1,0},{2,3},{3,2},{4,5},{5,4},{6,7},{7,6},{8,9},{9,8},{10,11... | collective-permute-start | bytes 3538952 | tf_op jit(solution)/shard_map/ppermute | solution.py:226
  1.8 12.7 %collective-permute-start.6 = (bf16[256,768]{1,0:T(8,128)(2,1)S(1)}, bf16[256,768]{1,0:T(8,128)(2,1)}, u32[]{:S(2)}, u32[]{:S(2)}) collective-permute-start(bf16[256,768]{1,0:T(8,128)(2,1)S(1)} %get-tuple-element.41), channel_id=1, source_target_pairs={{0,2},{2,0},{1,3},{3,1},{4,6},{6,4},{5,7},{7,5},{8,10},{10,8},{9,1... | collective-permute-start | bytes 1179656 | tf_op jit(solution)/shard_map/ppermute | solution.py:226
  4.4 22.7 %collective-permute-start.4 = (bf16[256,768]{1,0:T(8,128)(2,1)S(1)}, bf16[256,768]{1,0:T(8,128)(2,1)S(1)}, u32[]{:S(2)}, u32[]{:S(2)}) collective-permute-start(bf16[256,768]{1,0:T(8,128)(2,1)S(1)} %get-tuple-element.42), channel_id=1, source_target_pairs={{0,2},{2,0},{1,3},{3,1},{4,6},{6,4},{5,7},{7,5},{8,10},{10,8},{9,1... | collective-permute-start | bytes 1179656 | tf_op jit(solution)/shard_map/ppermute | solution.py:226
  5.2 21.9 %collective-permute-start.8 = (bf16[128,768]{1,0:T(8,128)(2,1)S(1)}, bf16[128,768]{1,0:T(8,128)(2,1)}, u32[]{:S(2)}, u32[]{:S(2)}) collective-permute-start(bf16[128,768]{1,0:T(8,128)(2,1)S(1)} %get-tuple-element.40), channel_id=1, source_target_pairs={{0,2},{2,0},{1,3},{3,1},{4,6},{6,4},{5,7},{7,5},{8,10},{10,8},{9,1... | collective-permute-start | bytes 589832 | tf_op jit(solution)/shard_map/ppermute | solution.py:226
  7.1 31.1 %collective-permute-start.10 = (bf16[128,768]{1,0:T(8,128)(2,1)}, bf16[128,768]{1,0:T(8,128)(2,1)S(1)}, u32[]{:S(2)}, u32[]{:S(2)}) collective-permute-start(bf16[128,768]{1,0:T(8,128)(2,1)} %get-tuple-element.39), channel_id=1, source_target_pairs={{0,2},{2,0},{1,3},{3,1},{4,6},{6,4},{5,7},{7,5},{8,10},{10,8},{9,1... | collective-permute-start | bytes 589832 | tf_op jit(solution)/shard_map/ppermute | solution.py:226
  14.4 14.5 %collective-permute-start.7 = (bf16[256,768]{1,0:T(8,128)(2,1)}, bf16[256,768]{1,0:T(8,128)(2,1)}, u32[]{:S(2)}, u32[]{:S(2)}) collective-permute-start(bf16[256,768]{1,0:T(8,128)(2,1)} %collective-permute-done.6.refs_2_), channel_id=1, source_target_pairs={{0,1},{1,0},{2,3},{3,2},{4,5},{5,4},{6,7},{7,6},{8,9},{9,8},{10,11... | collective-permute-start | bytes 1179656 | tf_op jit(solution)/shard_map/ppermute | solution.py:226
  27.1 12.6 %collective-permute-start.9 = (bf16[128,768]{1,0:T(8,128)(2,1)}, bf16[128,768]{1,0:T(8,128)(2,1)}, u32[]{:S(2)}, u32[]{:S(2)}) collective-permute-start(bf16[128,768]{1,0:T(8,128)(2,1)} %collective-permute-done.8.refs_2_), channel_id=1, source_target_pairs={{0,1},{1,0},{2,3},{3,2},{4,5},{5,4},{6,7},{7,6},{8,9},{9,8},{10,11... | collective-permute-start | bytes 589832 | tf_op jit(solution)/shard_map/ppermute | solution.py:226
  27.1 19.4 %collective-permute-start.5 = (bf16[256,768]{1,0:T(8,128)(2,1)S(1)}, bf16[256,768]{1,0:T(8,128)(2,1)S(1)}, u32[]{:S(2)}, u32[]{:S(2)}) collective-permute-start(bf16[256,768]{1,0:T(8,128)(2,1)S(1)} %collective-permute-done.4.refs_2_), channel_id=1, source_target_pairs={{0,1},{1,0},{2,3},{3,2},{4,5},{5,4},{6,7},{7,6},{8,9},{9,8},{10,11... | collective-permute-start | bytes 1179656 | tf_op jit(solution)/shard_map/ppermute | solution.py:226
  28.9 13.1 %collective-permute-start = (s32[2]{0:T(128)S(1)}, s32[2]{0:T(128)S(1)}, u32[]{:S(2)}, u32[]{:S(2)}) collective-permute-start(s32[2]{0:T(128)S(1)} %copy-done.9), channel_id=1, source_target_pairs={{0,4},{4,8},{8,12},{12,0},{1,5},{5,9},{9,13},{13,1},{2,6},{6,10},{... | collective-permute-start | bytes 32 | tf_op jit(solution)/shard_map/ppermute | solution.py:226
  30.9 11.7 %collective-permute-start.1 = (s32[2]{0:T(128)S(1)}, s32[2]{0:T(128)S(1)}, u32[]{:S(2)}, u32[]{:S(2)}) collective-permute-start(s32[2]{0:T(128)S(1)} %copy-done.9), channel_id=1, source_target_pairs={{0,8},{4,12},{8,0},{12,4},{1,9},{5,13},{9,1},{13,5},{2,10},{6,14},... | collective-permute-start | bytes 32 | tf_op jit(solution)/shard_map/ppermute | solution.py:226
  39.6 9.5 %collective-permute-start.11 = (bf16[128,768]{1,0:T(8,128)(2,1)S(1)}, bf16[128,768]{1,0:T(8,128)(2,1)S(1)}, u32[]{:S(2)}, u32[]{:S(2)}) collective-permute-start(bf16[128,768]{1,0:T(8,128)(2,1)S(1)} %collective-permute-done.10.refs_2_), channel_id=1, source_target_pairs={{0,1},{1,0},{2,3},{3,2},{4,5},{5,4},{6,7},{7,6},{8,9},{9,8},{10,11... | collective-permute-start | bytes 589832 | tf_op jit(solution)/shard_map/ppermute | solution.py:226
  42.0 9.7 %collective-permute-start.21 = (bf16[256,256]{1,0:T(8,128)(2,1)S(1)}, bf16[256,256]{1,0:T(8,128)(2,1)S(1)}, u32[]{:S(2)}, u32[]{:S(2)}) collective-permute-start(bf16[256,256]{1,0:T(8,128)(2,1)S(1)} %get-tuple-element.29.refs_5_), channel_id=1, source_target_pairs={{0,4},{4,8},{8,12},{12,0},{1,5},{5,9},{9,13},{13,1},{2,6},{6,10},{... | collective-permute-start | bytes 393224 | tf_op jit(solution)/shard_map/ppermute | solution.py:226
  42.7 9.0 %collective-permute-start.15 = (bf16[128,256]{1,0:T(8,128)(2,1)S(1)}, bf16[128,256]{1,0:T(8,128)(2,1)S(1)}, u32[]{:S(2)}, u32[]{:S(2)}) collective-permute-start(bf16[128,256]{1,0:T(8,128)(2,1)S(1)} %get-tuple-element.27.refs_6_), channel_id=1, source_target_pairs={{0,4},{4,8},{8,12},{12,0},{1,5},{5,9},{9,13},{13,1},{2,6},{6,10},{... | collective-permute-start | bytes 196616 | tf_op jit(solution)/shard_map/ppermute | solution.py:226
  42.9 14.4 %collective-permute-start.22 = (bf16[256,256]{1,0:T(8,128)(2,1)S(1)}, bf16[256,256]{1,0:T(8,128)(2,1)S(1)}, u32[]{:S(2)}, u32[]{:S(2)}) collective-permute-start(bf16[256,256]{1,0:T(8,128)(2,1)S(1)} %get-tuple-element.29.refs_5_), channel_id=1, source_target_pairs={{0,8},{4,12},{8,0},{12,4},{1,9},{5,13},{9,1},{13,5},{2,10},{6,14},... | collective-permute-start | bytes 393224 | tf_op jit(solution)/shard_map/ppermute | solution.py:226
  46.5 10.8 %collective-permute-start.23 = (bf16[256,256]{1,0:T(8,128)(2,1)S(1)}, bf16[256,256]{1,0:T(8,128)(2,1)S(1)}, u32[]{:S(2)}, u32[]{:S(2)}) collective-permute-start(bf16[256,256]{1,0:T(8,128)(2,1)S(1)} %get-tuple-element.29.refs_5_), channel_id=1, source_target_pairs={{0,12},{4,0},{8,4},{12,8},{1,13},{5,1},{9,5},{13,9},{2,14},{6,2},{... | collective-permute-start | bytes 393224 | tf_op jit(solution)/shard_map/ppermute | solution.py:226
  49.1 15.2 %collective-permute-start.18 = (bf16[256,256]{1,0:T(8,128)(2,1)S(1)}, bf16[256,256]{1,0:T(8,128)(2,1)S(1)}, u32[]{:S(2)}, u32[]{:S(2)}) collective-permute-start(bf16[256,256]{1,0:T(8,128)(2,1)S(1)} %get-tuple-element.28.refs_4_), channel_id=1, source_target_pairs={{0,4},{4,8},{8,12},{12,0},{1,5},{5,9},{9,13},{13,1},{2,6},{6,10},{... | collective-permute-start | bytes 393224 | tf_op jit(solution)/shard_map/ppermute | solution.py:226
  51.7 19.4 %collective-permute-start.19 = (bf16[256,256]{1,0:T(8,128)(2,1)S(1)}, bf16[256,256]{1,0:T(8,128)(2,1)S(1)}, u32[]{:S(2)}, u32[]{:S(2)}) collective-permute-start(bf16[256,256]{1,0:T(8,128)(2,1)S(1)} %get-tuple-element.28.refs_4_), channel_id=1, source_target_pairs={{0,8},{4,12},{8,0},{12,4},{1,9},{5,13},{9,1},{13,5},{2,10},{6,14},... | collective-permute-start | bytes 393224 | tf_op jit(solution)/shard_map/ppermute | solution.py:226
  51.7 21.0 %collective-permute-start.20 = (bf16[256,256]{1,0:T(8,128)(2,1)S(1)}, bf16[256,256]{1,0:T(8,128)(2,1)S(1)}, u32[]{:S(2)}, u32[]{:S(2)}) collective-permute-start(bf16[256,256]{1,0:T(8,128)(2,1)S(1)} %get-tuple-element.28.refs_4_), channel_id=1, source_target_pairs={{0,12},{4,0},{8,4},{12,8},{1,13},{5,1},{9,5},{13,9},{2,14},{6,2},{... | collective-permute-start | bytes 393224 | tf_op jit(solution)/shard_map/ppermute | solution.py:226
  57.3 23.1 %collective-permute-start.16 = (bf16[128,256]{1,0:T(8,128)(2,1)S(1)}, bf16[128,256]{1,0:T(8,128)(2,1)S(1)}, u32[]{:S(2)}, u32[]{:S(2)}) collective-permute-start(bf16[128,256]{1,0:T(8,128)(2,1)S(1)} %get-tuple-element.27.refs_6_), channel_id=1, source_target_pairs={{0,8},{4,12},{8,0},{12,4},{1,9},{5,13},{9,1},{13,5},{2,10},{6,14},... | collective-permute-start | bytes 196616 | tf_op jit(solution)/shard_map/ppermute | solution.py:226
  57.3 23.1 %collective-permute-start.17 = (bf16[128,256]{1,0:T(8,128)(2,1)S(1)}, bf16[128,256]{1,0:T(8,128)(2,1)S(1)}, u32[]{:S(2)}, u32[]{:S(2)}) collective-permute-start(bf16[128,256]{1,0:T(8,128)(2,1)S(1)} %get-tuple-element.27.refs_6_), channel_id=1, source_target_pairs={{0,12},{4,0},{8,4},{12,8},{1,13},{5,1},{9,5},{13,9},{2,14},{6,2},{... | collective-permute-start | bytes 196616 | tf_op jit(solution)/shard_map/ppermute | solution.py:226
  64.3 18.1 %collective-permute-start.12 = (bf16[128,256]{1,0:T(8,128)(2,1)S(1)}, bf16[128,256]{1,0:T(8,128)(2,1)S(1)}, u32[]{:S(2)}, u32[]{:S(2)}) collective-permute-start(bf16[128,256]{1,0:T(8,128)(2,1)S(1)} %get-tuple-element.26.refs_7_), channel_id=1, source_target_pairs={{0,4},{4,8},{8,12},{12,0},{1,5},{5,9},{9,13},{13,1},{2,6},{6,10},{... | collective-permute-start | bytes 196616 | tf_op jit(solution)/shard_map/ppermute | solution.py:226
  71.1 11.4 %collective-permute-start.13 = (bf16[128,256]{1,0:T(8,128)(2,1)S(1)}, bf16[128,256]{1,0:T(8,128)(2,1)S(1)}, u32[]{:S(2)}, u32[]{:S(2)}) collective-permute-start(bf16[128,256]{1,0:T(8,128)(2,1)S(1)} %get-tuple-element.26.refs_7_), channel_id=1, source_target_pairs={{0,8},{4,12},{8,0},{12,4},{1,9},{5,13},{9,1},{13,5},{2,10},{6,14},... | collective-permute-start | bytes 196616 | tf_op jit(solution)/shard_map/ppermute | solution.py:226
  72.6 9.8 %collective-permute-start.14 = (bf16[128,256]{1,0:T(8,128)(2,1)S(1)}, bf16[128,256]{1,0:T(8,128)(2,1)S(1)}, u32[]{:S(2)}, u32[]{:S(2)}) collective-permute-start(bf16[128,256]{1,0:T(8,128)(2,1)S(1)} %get-tuple-element.26.refs_7_), channel_id=1, source_target_pairs={{0,12},{4,0},{8,4},{12,8},{1,13},{5,1},{9,5},{13,9},{2,14},{6,2},{... | collective-permute-start | bytes 196616 | tf_op jit(solution)/shard_map/ppermute | solution.py:226
  84.6 5.7 %collective-permute-start.25 = (bf16[768,128]{1,0:T(8,128)(2,1)S(1)}, bf16[768,128]{1,0:T(8,128)(2,1)S(1)}, u32[]{:S(2)}, u32[]{:S(2)}) collective-permute-start(bf16[768,128]{1,0:T(8,128)(2,1)S(1)} %shard_map.107.refs_0_), channel_id=1, source_target_pairs={{0,2},{2,0},{1,3},{3,1},{4,6},{6,4},{5,7},{7,5},{8,10},{10,8},{9,1... | collective-permute-start | bytes 589832 | tf_op jit(solution)/shard_map/ppermute | solution.py:226
  (13 other events, 181.4 us)
